TPU v7x, 32 devices: a whole 2x2x4 slice. The times are simulated.
32 devices in a mesh: chan: 4 (over y, core), rng: 8 (over z, x).
Axes of the slice: x: 2, y: 2, z: 4, core: 2. Of those that a mesh axis runs over, the one named last changes fastest.
Arguments:
- echoes: float32 [2, 512, 64, 1024], P(None, 'chan', None, 'rng'), may hold values from -6 to 6
- filter_taps: float32 [2, 512], replicated, may hold values from -0.1875 to 0.1875
Outputs:
- covariance: float32 [2, 64, 512, 512], P(None, 'rng', 'chan')
All inputs are finite; a program needn't handle non-finite values.
Results may differ from a plain program's by a relative error of at most 0.0003.
Values sent between devices are 32-bit elements; how exact they have to be, the bound alone decides.
A program may use at most 128 MiB of HBM per device.

v0:
```python
import math

import jax
import jax.numpy as jnp
from jax import lax
from jax.sharding import PartitionSpec as P


def toeplitz(pattern_row, span, window, tap_count):
    pattern = jnp.concatenate([pattern_row, jnp.zeros((window + 1 - tap_count,), jnp.float32)])
    return jnp.tile(pattern, span)[: span * window].reshape(span, window)


def range_filter(block_data, filter_taps):
    gate_count = block_data.shape[3]
    tap_count = filter_taps.shape[1]
    span = min(512, gate_count)
    blocks = gate_count // span
    extent = 1 + (tap_count + span - 2) // span
    window = extent * span
    padded = jnp.pad(block_data, ((0, 0), (0, 0), (0, 0), (0, (extent - 1) * span)))
    shaped = padded.reshape(block_data.shape[:3] + (blocks + extent - 1, span))
    windows = jnp.concatenate(
        [shaped[:, :, :, offset : offset + blocks, :] for offset in range(extent)], axis=4
    )
    toep_re = toeplitz(filter_taps[0], span, window, tap_count)
    toep_im = toeplitz(filter_taps[1], span, window, tap_count)
    joined = jnp.concatenate([windows[0], windows[1]], axis=3)
    table_re = jnp.concatenate([toep_re, -toep_im], axis=1)
    table_im = jnp.concatenate([toep_im, toep_re], axis=1)
    both_tables = jnp.stack([table_re, table_im])
    result = jnp.einsum(
        "abnw,sow->sabno",
        joined,
        both_tables,
        precision=lax.Precision.HIGHEST,
        preferred_element_type=jnp.float32,
    )
    return result.reshape(block_data.shape)


def doppler(block_data):
    pulse_count = block_data.shape[2]
    pulse_idx = jnp.arange(pulse_count, dtype=jnp.int32)
    phases = (pulse_idx[:, None] * pulse_idx[None, :] % pulse_count).astype(jnp.float32) * (
        2.0 * math.pi / pulse_count
    )
    cos_table = jnp.cos(phases)
    sin_table = jnp.sin(phases)
    norm_factor = 1.0 / math.sqrt(pulse_count)

    def contract(part_data, table):
        return jnp.einsum(
            "cpg,pd->cdg",
            part_data,
            table,
            precision=lax.Precision.HIGHEST,
            preferred_element_type=jnp.float32,
        )

    spec_re = (
        contract(block_data[0], cos_table) + contract(block_data[1], sin_table)
    ) * norm_factor
    spec_im = (
        contract(block_data[1], cos_table) - contract(block_data[0], sin_table)
    ) * norm_factor
    return jnp.stack([spec_re, spec_im])


def products(left_part, right_part):
    return jnp.einsum(
        "akg,bkg->kab",
        left_part,
        right_part,
        precision=lax.Precision.HIGHEST,
        preferred_element_type=jnp.float32,
    )


def per_device(echoes, filter_taps):
    rng_count = lax.axis_size("rng")
    gate_count = echoes.shape[3] * rng_count
    by_range = lax.all_to_all(echoes, "rng", split_axis=2, concat_axis=3, tiled=True)
    filtered = range_filter(by_range, filter_taps)
    by_pulse = lax.all_to_all(filtered, "rng", split_axis=3, concat_axis=2, tiled=True)
    spectrum = doppler(by_pulse)
    by_bins = lax.all_to_all(spectrum, "rng", split_axis=2, concat_axis=3, tiled=True)
    gathered = lax.all_to_all(by_bins, "chan", split_axis=3, concat_axis=1, tiled=True)
    spec_re = gathered[0]
    spec_im = gathered[1]
    joined = jnp.concatenate([spec_re, spec_im], axis=2)
    turned = jnp.concatenate([spec_im, -spec_re], axis=2)
    real_part = products(joined, joined) / gate_count
    imag_part = products(turned, joined) / gate_count
    summed = (
        lax.psum_scatter(real_part, "chan", scatter_dimension=1, tiled=True),
        lax.psum_scatter(imag_part, "chan", scatter_dimension=1, tiled=True),
    )
    return jnp.stack([summed[0], summed[1]])


def solution(mesh):
    in_specs = (P(None, "chan", None, "rng"), P())
    out_specs = P(None, "rng", "chan", None)
    return jax.shard_map(
        per_device, mesh=mesh, in_specs=in_specs, out_specs=out_specs, check_vma=False
    )
```

profile of v0, /device:TPU:0, one launch (start us, length us, event | category | flops | bytes accessed | tf_op | source)
XLA Modules:
  0.0 1033.5 jit_solution(12534578767438191888)
XLA Ops:
  6.5 11.5 %copy.11 = f32[2,128,64,128]{3,1,0,2:T(8,128)} copy(f32[2,128,64,128]{3,2,1,0:T(8,128)} %param.2) | data formatting | bytes 16777216 | tf_op args[0]
  18.0 7.4 all-to-all-start
  45.7 7.3 maximum_bitcast_fusion.4
  53.0 155.6 %all-to-all-done = f32[2,128,64,128]{3,1,0,2:T(8,128)} async-done(((f32[2,128,64,128]{3,1,0,2:T(8,128)}), f32[2,128,64,128]{3,1,0,2:T(8,128)}, u32[]{:S(2)}, u32[]{:S(2)}) %all-to-all-start) | async-done | bytes 8388640 | tf_op jit(solution)/shard_map/all_to_all | solution.py:83
  208.6 8.7 copy.12
  217.2 5.0 pad.6
  222.3 6.3 fusion.54
  228.6 8.7 copy.23
  237.3 8.7 copy.24
  246.0 11.5 %fusion.4 = (f32[128,8,2,1024]{3,0,2,1:T(8,128)}, f32[128,8,2,1024]{3,0,2,1:T(8,128)}) fusion(f32[2,128,8,2,512]{4,1,3,2,0:T(8,128)} %copy.23, f32[2,128,8,2,512]{4,1,3,2,0:T(8,128)} %copy.24), kind=kLoop, calls=%fused_computation.7 | loop fusion | flops 4194304 | bytes 33554432 | tf_op jit(solution)/shard_map/squeeze | solution.py:28
  257.5 62.0 %fusion = f32[2,512,128,8,2]{2,1,4,3,0:T(8,128)S(1)} fusion(f32[128,8,2,1024]{3,0,2,1:T(8,128)} %get-tuple-element.6, f32[128,8,2,1024]{3,0,2,1:T(8,128)} %get-tuple-element.5, f32[1,512,2048]{2,1,0:T(8,128)} %get-tuple-element.12, f32[1,512,2048]{2,1,0:T(8,128)S(1)} %copy-done.3), kind=kOutput, calls=%fused_computation.3 | convolution fusion | flops 51545899008 | bytes 33554432 | tf_op jit(solution)/shard_map/abnw,sow->sabno/dot_general | solution.py:32
  319.5 4.9 copy.15
  324.4 186.7 %all_to_all.66 = f32[2,128,8,1024]{1,2,0,3:T(8,128)} all-to-all(f32[2,128,8,1024]{1,2,0,3:T(8,128)S(1)} %copy.15), channel_id=1, replica_groups=mesh['chan'=4,'rng'=8] {'rng'}, dimensions={3} | all-to-all | bytes 16777216 | tf_op jit(solution)/shard_map/all_to_all | solution.py:85
  511.1 8.7 copy.16
  519.8 6.1 fusion.13
  545.7 186.7 %all_to_all.67 = f32[2,128,64,128]{3,1,0,2:T(8,128)} all-to-all(f32[2,128,64,128]{3,1,0,2:T(8,128)S(1)} %copy.17), channel_id=1, replica_groups=mesh['chan'=4,'rng'=8] {'rng'}, dimensions={2} | all-to-all | bytes 16777216 | tf_op jit(solution)/shard_map/all_to_all | solution.py:87
  732.4 9.2 copy.18
  741.6 97.5 %all_to_all.68 = f32[2,128,8,1024]{1,2,0,3:T(8,128)S(1)} all-to-all(f32[2,128,8,1024]{1,2,0,3:T(8,128)} %bitcast.89), channel_id=1, replica_groups=mesh['chan'=4,'rng'=8] {'chan'}, dimensions={3} | all-to-all | bytes 16777216 | tf_op jit(solution)/shard_map/all_to_all | solution.py:88
  845.7 5.4 copy.21
  851.1 5.4 copy.20
  861.2 16.1 %broadcast_multiply_fusion = f32[8,512,512]{2,1,0:T(8,128)} fusion(f32[512,8,256]{2,0,1:T(8,128)S(1)} %bitcast.81, f32[512,8,256]{2,0,1:T(8,128)S(1)} %bitcast.84, f32[512,8,256]{2,0,1:T(8,128)S(1)} %neg.7), kind=kOutput, calls=%fused_computation.25 | convolution fusion | flops 12891193344 | bytes 20971520 | tf_op jit(solution)/shard_map/akg,bkg->kab/dot_general | solution.py:71
  877.3 21.2 %broadcast_multiply_fusion.1 = f32[8,512,512]{2,1,0:T(8,128)} fusion(f32[512,8,256]{2,0,1:T(8,128)} %bitcast.80, f32[512,8,256]{2,0,1:T(8,128)} %bitcast.83), kind=kOutput, calls=%fused_computation.26 | convolution fusion | flops 12889096192 | bytes 16777216 | tf_op jit(solution)/shard_map/akg,bkg->kab/dot_general | solution.py:71
  898.5 48.3 %reduce-scatter.5.cloned.1.call-done = f32[8,128,512]{2,1,0:T(8,128)} async-done(((f32[8,512,512]{2,1,0:T(8,128)}), f32[8,128,512]{2,1,0:T(8,128)}) %reduce-scatter.5.cloned.1.call-update) | async-done | bytes 2097168 | tf_op jit(solution)/shard_map/reduce_scatter | solution.py:97
  946.8 74.5 %reduce-scatter.3.cloned.1.call-done = f32[8,128,512]{2,1,0:T(8,128)} async-done(((f32[8,512,512]{2,1,0:T(8,128)}), f32[8,128,512]{2,1,0:T(8,128)}) %reduce-scatter.3.cloned.1.call-update) | async-done | bytes 2097168 | tf_op jit(solution)/shard_map/reduce_scatter | solution.py:96
  (35 shorter events, 56.2 us)
Async XLA Ops:
  18.0 7.6 copy-start.4
  18.0 190.6 %all-to-all-start = ((f32[2,128,64,128]{3,1,0,2:T(8,128)}), f32[2,128,64,128]{3,1,0,2:T(8,128)}, u32[]{:S(2)}, u32[]{:S(2)}) async-start(f32[2,128,64,128]{3,1,0,2:T(8,128)} %copy.11), calls=%async_computation | async-start | bytes 16777216 | tf_op jit(solution)/shard_map/all_to_all | solution.py:83
  25.4 921.4 %reduce-scatter.5.cloned.1.call-start = ((), (), s32[]{:S(2)}) async-start(), calls=%async_computation.7 | async-start | bytes 10485760 | tf_op jit(solution)/shard_map/reduce_scatter | solution.py:97
  246.0 11.5 %copy-start.3 = (f32[1,512,2048]{2,1,0:T(8,128)S(1)}, f32[1,512,2048]{2,1,0:T(8,128)}, u32[]{:S(2)}) copy-start(f32[1,512,2048]{2,1,0:T(8,128)} %get-tuple-element.11) | copy-start | bytes 12582916
  519.8 6.1 copy-start
  856.4 3.4 copy-start.1
  856.4 4.7 copy-start.2
  877.3 144.0 %reduce-scatter.3.cloned.1.call-start = ((), (), s32[]{:S(2)}) async-start(), calls=%async_computation.6 | async-start | bytes 10485760 | tf_op jit(solution)/shard_map/reduce_scatter | solution.py:96
Sparse Core Ops, SparseCore 0:
  877.4 69.3 reduce-scatter.4
  949.6 71.7 reduce-scatter.2
where the time goes:
time: 1040 us; the launch traced here: 1030 us
  blocking collectives  471 us (45%)
  waiting for transfers between devices  278 us (27%)
  matrix products  119 us (11%)
  local copies, waits for them, and re-layouts  114 us (11%)
  other arithmetic  29.5 us (3%)
  between operations  14.1 us (1%)
    all_to_all x1, blocking collectives, per_device(): lax.all_to_all(filtered, 'rng', split_axis=3, concat_axis=2, tiled=True)  187 us
    all_to_all x1, blocking collectives, per_device(): lax.all_to_all(spectrum, 'rng', split_axis=2, concat_axis=3, tiled=True)  187 us
    all_to_all x1, waiting for transfers between devices, per_device(): lax.all_to_all(echoes, 'rng', split_axis=2, concat_axis=3, tiled=True)  156 us
    all_to_all x1, blocking collectives, per_device(): lax.all_to_all(by_bins, 'chan', split_axis=3, concat_axis=1, tiled=True)  97.5 us
    reduce_scatter x1, waiting for transfers between devices, per_device(): lax.psum_scatter(real_part, 'chan', scatter_dimension=1, tiled=True)  74.5 us
    dot_general x1, matrix products, range_filter(): jnp.einsum('abnw,sow->sabno', joined, both_tables, precision=lax.Precisio...  62 us
    reduce_scatter x1, waiting for transfers between devices, per_device(): lax.psum_scatter(imag_part, 'chan', scatter_dimension=1, tiled=True)  48.3 us
    dot_general x2, matrix products, products(): jnp.einsum('akg,bkg->kab', left_part, right_part, precision=lax.Precision...  37.3 us
  transfers between devices with their start and end apart: 3, of which 3 were waited for; matrix products, arithmetic and copies ran while one was open for 5% of the time, Pallas kernels for 0%

commit v1 on v0

--- a/solution.py
+++ b/solution.py
@@ -77,15 +77,12 @@
     )
 
 
-def per_device(echoes, filter_taps):
+def by_gates(echoes, filter_taps):
     rng_count = lax.axis_size("rng")
     gate_count = echoes.shape[3] * rng_count
-    by_range = lax.all_to_all(echoes, "rng", split_axis=2, concat_axis=3, tiled=True)
-    filtered = range_filter(by_range, filter_taps)
-    by_pulse = lax.all_to_all(filtered, "rng", split_axis=3, concat_axis=2, tiled=True)
-    spectrum = doppler(by_pulse)
-    by_bins = lax.all_to_all(spectrum, "rng", split_axis=2, concat_axis=3, tiled=True)
-    gathered = lax.all_to_all(by_bins, "chan", split_axis=3, concat_axis=1, tiled=True)
+    by_bins = lax.all_to_all(doppler(echoes), "rng", split_axis=2, concat_axis=3, tiled=True)
+    filtered = range_filter(by_bins, filter_taps)
+    gathered = lax.all_to_all(filtered, "chan", split_axis=3, concat_axis=1, tiled=True)
     spec_re = gathered[0]
     spec_im = gathered[1]
     joined = jnp.concatenate([spec_re, spec_im], axis=2)
@@ -99,7 +96,91 @@
     return jnp.stack([summed[0], summed[1]])
 
 
+def doppler_table(pulse_count):
+    idx = jnp.arange(pulse_count, dtype=jnp.int32)
+    phases = (idx[:, None] * idx[None, :] % pulse_count).astype(jnp.float32) * (
+        2.0 * math.pi / pulse_count
+    )
+    norm_factor = 1.0 / math.sqrt(pulse_count)
+    cos_table = jnp.cos(phases) * norm_factor
+    sin_table = jnp.sin(phases) * norm_factor
+    return jnp.stack(
+        [jnp.stack([cos_table, sin_table]), jnp.stack([-sin_table, cos_table])]
+    )
+
+
+def by_bins(echoes, filter_taps):
+    rng_count = lax.axis_size("rng")
+    chan_count = lax.axis_size("chan")
+    channels, pulse_count, part = echoes.shape[1:]
+    gate_count = part * rng_count
+    tap_count = filter_taps.shape[1]
+    own = pulse_count // (rng_count * chan_count)
+    table = doppler_table(pulse_count)
+    spectrum = jnp.einsum(
+        "tspd,scpg->dtcg",
+        table,
+        echoes,
+        precision=lax.Precision.HIGH,
+        preferred_element_type=jnp.float32,
+    )
+    arrived = lax.all_to_all(spectrum, ("rng", "chan"), split_axis=0, concat_axis=0, tiled=True)
+    arrived = arrived.reshape(rng_count, chan_count, own, 2, channels, part)
+    samples = arrived.transpose(2, 1, 4, 3, 0, 5).reshape(
+        own, chan_count * channels, 2, gate_count
+    )
+    span = gate_count // 2
+    window = gate_count
+    toep_re = toeplitz(filter_taps[0], span, window, tap_count).T
+    toep_im = toeplitz(filter_taps[1], span, window, tap_count).T
+    weights = jnp.stack(
+        [jnp.stack([toep_re, toep_im]), jnp.stack([-toep_im, toep_re])]
+    )
+
+    def convolve(data, tables):
+        return jnp.einsum(
+            "bctg,tugx->bcux",
+            data,
+            tables,
+            precision=lax.Precision.HIGH,
+            preferred_element_type=jnp.float32,
+        )
+
+    halves = [
+        convolve(samples, weights),
+        convolve(samples[..., span:], weights[:, :, :span]),
+    ]
+
+    def correlate(left_part, right_part):
+        return jnp.einsum(
+            "bag,bcg->bac",
+            left_part,
+            right_part,
+            precision=lax.Precision.HIGH,
+            preferred_element_type=jnp.float32,
+        )
+
+    real_part = 0.0
+    cross = 0.0
+    for half in halves:
+        flat = half.reshape(own, chan_count * channels, 2 * span)
+        real_part = real_part + correlate(flat, flat)
+        cross = cross + correlate(half[:, :, 1], half[:, :, 0])
+    imag_part = cross - cross.transpose(0, 2, 1)
+    both = jnp.stack([real_part, imag_part]) / gate_count
+    return lax.all_to_all(both, "chan", split_axis=2, concat_axis=1, tiled=True)
+
+
 def solution(mesh):
+    devices = mesh.shape["rng"] * mesh.shape["chan"]
+
+    def per_device(echoes, filter_taps):
+        gate_count = echoes.shape[3] * mesh.shape["rng"]
+        whole_bins = echoes.shape[2] % devices == 0
+        if whole_bins and gate_count == 2 * filter_taps.shape[1]:
+            return by_bins(echoes, filter_taps)
+        return by_gates(echoes, filter_taps)
+
     in_specs = (P(None, "chan", None, "rng"), P())
     out_specs = P(None, "rng", "chan", None)
     return jax.shard_map(

time: 1040 us -> 349 us (0.34)
  the two profiles are of different devices: /device:TPU:0 before, /device:TPU:2 now
where the time goes in v1:
time: 349 us; the launch traced here: 342 us
  waiting for transfers between devices  166 us (48%)
  local copies, waits for them, and re-layouts  65 us (19%)
  blocking collectives  54.6 us (16%)
  matrix products  42 us (12%)
  other arithmetic  7.62 us (2%)
  starting transfers between devices  6.55 us (2%)
    all_to_all x1, waiting for transfers between devices, by_bins(): lax.all_to_all(spectrum, ('rng', 'chan'), split_axis=0, concat_axis=0, ti...  166 us
    all_to_all x1, blocking collectives, by_bins(): return lax.all_to_all(both, 'chan', split_axis=2, concat_axis=1, tiled=True)  54.6 us
    dot_general x2, matrix products, convolve(): jnp.einsum('bctg,tugx->bcux', data, tables, precision=lax.Precision.HIGH,...  24.6 us
    reshape x2, local copies, waits for them, and re-layouts, by_bins(): arrived.transpose(2, 1, 4, 3, 0, 5)  18.6 us
    reshape x1, local copies, waits for them, and re-layouts, by_bins(): arrived = arrived.reshape(rng_count, chan_count, own, 2, channels, part)  13.2 us
    dot_general x4, matrix products, correlate(): jnp.einsum('bag,bcg->bac', left_part, right_part, precision=lax.Precision...  11.1 us
    transpose x1, local copies, waits for them, and re-layouts, by_bins(): jnp.einsum('tspd,scpg->dtcg', table, echoes, precision=lax.Precision.HIGH...  8.1 us
  transfers between devices with their start and end apart: 1, of which 1 were waited for; matrix products, arithmetic and copies ran while one was open for 5% of the time, Pallas kernels for 0%

profile of v1, /device:TPU:2, one launch (start us, length us, event | category | flops | bytes accessed | tf_op | source)
XLA Modules:
  0.0 342.3 jit_solution(16925415731025082099)
XLA Ops:
  0.3 6.4 %fusion.11 = f32[64,2,128,128]{3,0,2,1:T(8,128)S(1)} fusion(f32[2,128,64,128]{3,2,1,0:T(8,128)} %param.2, f32[1,2,64,64]{2,3,1,0:T(8,128)S(1)} %get-tuple-element.8, f32[1,2,64,64]{2,3,1,0:T(8,128)S(1)} %get-tuple-element.7), kind=kOutput, calls=%fused_computation.17 | convolution fusion | flops 1610629120 | bytes 16842752 | tf_op jit(solution)/shard_map/tspd,scpg->dtcg/dot_general | solution.py:120
  6.7 8.1 %copy.34 = f32[64,2,128,128]{3,2,1,0:T(8,128)} copy(f32[64,2,128,128]{3,0,2,1:T(8,128)S(1)} %fusion.11) | data formatting | bytes 16777216 | tf_op jit(solution)/shard_map/tspd,scpg->dtcg/transpose | solution.py:120
  14.8 6.5 %all-to-all-start = ((f32[64,2,128,128]{3,2,1,0:T(8,128)}), f32[64,2,128,128]{3,2,1,0:T(8,128)}, u32[]{:S(2)}, u32[]{:S(2)}) async-start(f32[64,2,128,128]{3,2,1,0:T(8,128)} %copy.34), calls=%async_computation | async-start | bytes 16777216 | tf_op jit(solution)/shard_map/all_to_all | solution.py:127
  21.6 2.3 tile.9
  27.1 2.3 tile.21
  29.4 3.1 slice.41
  32.5 1.7 reshape.107
  35.8 4.3 %maximum_bitcast_fusion.1 = (f32[1,2,1024,512]{2,3,0,1:T(8,128)}, f32[1,2,1024,512]{2,3,0,1:T(8,128)}) fusion(f32[1,1024,512]{1,2,0:T(8,128)S(1)} %bitcast.112, f32[1,1024,512]{1,2,0:T(8,128)S(1)} %fusion.17, f32[1,1024,512]{1,2,0:T(8,128)S(1)} %bitcast.110), kind=kLoop, calls=%fused_computation.15 | loop fusion | flops 2097152 | bytes 14680064 | tf_op jit(solution)/shard_map/stack | solution.py:136
  40.1 166.0 %all-to-all-done = f32[64,2,128,128]{3,2,1,0:T(8,128)} async-done(((f32[64,2,128,128]{3,2,1,0:T(8,128)}), f32[64,2,128,128]{3,2,1,0:T(8,128)}, u32[]{:S(2)}, u32[]{:S(2)}) %all-to-all-start) | async-done | bytes 8388640 | tf_op jit(solution)/shard_map/all_to_all | solution.py:127
  206.1 13.2 %copy.73 = f32[8,4,2,2,128,128]{5,0,4,1,3,2:T(8,128)} copy(f32[8,4,2,2,128,128]{5,4,3,2,1,0:T(8,128)} %bitcast.8) | data formatting | bytes 16777216 | tf_op jit(solution)/shard_map/reshape | solution.py:128
  219.3 9.3 %reshape.113 = f32[2,512,2,1024,1]{3,1,2,0,4:T(8,128)} reshape(f32[2,4,128,2,8,128]{5,4,2,1,3,0:T(8,128)} %bitcast.104) | data formatting | bytes 16777216 | tf_op jit(solution)/shard_map/reshape | solution.py:129
  228.6 9.3 %reshape.105 = f32[2,512,2,1024]{3,1,2,0:T(8,128)} reshape(f32[2,4,128,2,8,128]{5,4,2,1,3,0:T(8,128)} %bitcast.105) | data formatting | bytes 16777216 | tf_op jit(solution)/shard_map/reshape | solution.py:129
  237.9 17.7 %fusion.1 = f32[2,512,2,512,1]{1,3,4,2,0:T(8,128)S(1)} fusion(f32[1,2,1024,512]{2,3,0,1:T(8,128)} %get-tuple-element.5, f32[1,2,1024,512]{2,3,0,1:T(8,128)} %get-tuple-element.6, f32[2,512,2,1024,1]{3,1,2,0,4:T(8,128)} %reshape.113), kind=kOutput, calls=%fused_computation.4 | convolution fusion | flops 12886999040 | bytes 20971520 | tf_op jit(solution)/shard_map/bctg,tugx->bcux/dot_general | solution.py:141
  255.6 6.9 %fusion.9 = f32[2,512,2,512,1]{1,3,4,2,0:T(8,128)S(1)} fusion(f32[1,2,1024,512]{2,3,0,1:T(8,128)S(1)} %copy-done.6, f32[1,2,1024,512]{2,3,0,1:T(8,128)S(1)} %copy-done.5, f32[2,512,2,1024]{3,1,2,0:T(8,128)S(1)} %copy-done.4), kind=kOutput, calls=%fused_computation.12 | convolution fusion | flops 6443499520 | bytes 16777216 | tf_op jit(solution)/shard_map/bctg,tugx->bcux/dot_general | solution.py:141
  262.5 2.0 copy-done
  264.5 1.9 fusion.14
  266.3 1.9 fusion.18
  268.3 2.0 copy.47
  270.3 2.2 fusion.16
  273.1 3.6 %fusion.32 = f32[2,512,512]{2,1,0:T(8,128)S(1)} fusion(f32[2,512,1024]{1,2,0:T(8,128)S(1)} %bitcast.109), kind=kOutput, calls=%fused_computation.51 | convolution fusion | flops 3221225472 | bytes 6291456 | tf_op jit(solution)/shard_map/bag,bcg->bac/dot_general | solution.py:155
  276.8 3.7 %add_bitcast_fusion = f32[1,2,512,512]{3,2,1,0:T(8,128)S(1)} fusion(f32[2,512,512]{2,1,0:T(8,128)S(1)} %fusion.32, f32[2,512,1024]{1,2,0:T(8,128)S(1)} %bitcast.107), kind=kOutput, calls=%fused_computation.28 | convolution fusion | flops 3221749760 | bytes 8388608 | tf_op jit(solution)/shard_map/bag,bcg->bac/dot_general | solution.py:155
  281.0 3.2 copy.48
  284.2 54.6 %all_to_all.23 = f32[2,2,512,512]{3,1,0,2:T(2,128)S(1)} all-to-all(f32[2,2,512,512]{3,1,0,2:T(2,128)S(1)} %copy.48), channel_id=1, replica_groups=mesh['chan'=4,'rng'=8] {'chan'}, dimensions={2} | all-to-all | bytes 8388608 | tf_op jit(solution)/shard_map/all_to_all | solution.py:171
  338.8 3.3 copy.49
  (30 shorter events, 6.4 us)
Async XLA Ops:
  14.8 6.6 %copy-start.8 = (f32[2,512]{1,0:T(2,128)S(1)}, f32[2,512]{1,0:T(2,128)}, u32[]{:S(2)}) copy-start(f32[2,512]{1,0:T(2,128)} %param.3) | copy-start | bytes 12292
  14.8 191.3 %all-to-all-start = ((f32[64,2,128,128]{3,2,1,0:T(8,128)}), f32[64,2,128,128]{3,2,1,0:T(8,128)}, u32[]{:S(2)}, u32[]{:S(2)}) async-start(f32[64,2,128,128]{3,2,1,0:T(8,128)} %copy.34), calls=%async_computation | async-start | bytes 16777216 | tf_op jit(solution)/shard_map/all_to_all | solution.py:127
  23.9 1.6 slice-start
  34.2 1.6 copy-start.7
  237.9 17.7 %copy-start.4 = (f32[2,512,2,1024]{3,1,2,0:T(8,128)S(1)}, f32[2,512,2,1024]{3,1,2,0:T(8,128)}, u32[]{:S(2)}) copy-start(f32[2,512,2,1024]{3,1,2,0:T(8,128)} %reshape.105) | copy-start | bytes 25165828
  237.9 17.7 %copy-start.5 = (f32[1,2,1024,512]{2,3,0,1:T(8,128)S(1)}, f32[1,2,1024,512]{2,3,0,1:T(8,128)}, u32[]{:S(2)}) copy-start(f32[1,2,1024,512]{2,3,0,1:T(8,128)} %get-tuple-element.5) | copy-start | bytes 12582916
  237.9 17.7 %copy-start.6 = (f32[1,2,1024,512]{2,3,0,1:T(8,128)S(1)}, f32[1,2,1024,512]{2,3,0,1:T(8,128)}, u32[]{:S(2)}) copy-start(f32[1,2,1024,512]{2,3,0,1:T(8,128)} %get-tuple-element.6) | copy-start | bytes 12582916
  255.6 10.7 %copy-start.2 = (f32[2,512,2,512,1]{1,3,4,2,0:T(8,128)}, f32[2,512,2,512,1]{1,3,4,2,0:T(8,128)S(1)}, u32[]{:S(2)}) copy-start(f32[2,512,2,512,1]{1,3,4,2,0:T(8,128)S(1)} %fusion.1) | copy-start | bytes 12582916
  262.5 2.0 copy-start
  270.3 2.8 copy-start.3
  273.1 3.6 %copy-start.1 = (f32[2,512,2,512,1]{1,3,4,2,0:T(8,128)S(1)}, f32[2,512,2,512,1]{1,3,4,2,0:T(8,128)}, u32[]{:S(2)}) copy-start(f32[2,512,2,512,1]{1,3,4,2,0:T(8,128)} %copy-done) | copy-start | bytes 12582916

commit v2 on v0

--- a/solution.py
+++ b/solution.py
@@ -1,8 +1,13 @@
+import functools
 import math
 
 import jax
 import jax.numpy as jnp
+import ml_dtypes
+import numpy as np
 from jax import lax
+from jax.experimental import pallas as pl
+from jax.experimental.pallas import tpu as pltpu
 from jax.sharding import PartitionSpec as P
 
 
@@ -77,15 +82,12 @@
     )
 
 
-def per_device(echoes, filter_taps):
+def by_gates(echoes, filter_taps):
     rng_count = lax.axis_size("rng")
     gate_count = echoes.shape[3] * rng_count
-    by_range = lax.all_to_all(echoes, "rng", split_axis=2, concat_axis=3, tiled=True)
-    filtered = range_filter(by_range, filter_taps)
-    by_pulse = lax.all_to_all(filtered, "rng", split_axis=3, concat_axis=2, tiled=True)
-    spectrum = doppler(by_pulse)
-    by_bins = lax.all_to_all(spectrum, "rng", split_axis=2, concat_axis=3, tiled=True)
-    gathered = lax.all_to_all(by_bins, "chan", split_axis=3, concat_axis=1, tiled=True)
+    by_bins = lax.all_to_all(doppler(echoes), "rng", split_axis=2, concat_axis=3, tiled=True)
+    filtered = range_filter(by_bins, filter_taps)
+    gathered = lax.all_to_all(filtered, "chan", split_axis=3, concat_axis=1, tiled=True)
     spec_re = gathered[0]
     spec_im = gathered[1]
     joined = jnp.concatenate([spec_re, spec_im], axis=2)
@@ -99,7 +101,316 @@
     return jnp.stack([summed[0], summed[1]])
 
 
+SPAN = 256
+LANES = 128
+PIECES = 2
+MIB = 2**20
+
+
+def doppler_table(pulse_count):
+    idx = np.arange(pulse_count)
+    phases = 2.0 * np.pi * (idx[:, None] * idx[None, :] % pulse_count) / pulse_count
+    cos_table = np.cos(phases) / math.sqrt(pulse_count)
+    sin_table = np.sin(phases) / math.sqrt(pulse_count)
+    rows = np.stack(
+        [
+            np.concatenate([cos_table, sin_table], axis=1),
+            np.concatenate([-sin_table, cos_table], axis=1),
+        ],
+        axis=1,
+    )
+    table = rows.reshape(2 * pulse_count, 2 * pulse_count).astype(np.float32)
+    high = table.astype(ml_dtypes.bfloat16)
+    low = (table - high.astype(np.float32)).astype(ml_dtypes.bfloat16)
+    return np.concatenate([high, low, high], axis=1)
+
+
+def halves_of(values):
+    high = values.astype(jnp.bfloat16)
+    low = (values - high.astype(jnp.float32)).astype(jnp.bfloat16)
+    return high, low
+
+
+def dot_rows(left, right):
+    return lax.dot_general(
+        left, right, (((1,), (1,)), ((), ())), preferred_element_type=jnp.float32
+    )
+
+
+def band_kernel(taps_ref, high_ref, low_ref):
+    tap_count = taps_ref.shape[1]
+    width = tap_count + SPAN
+    bands = []
+    for part in range(2):
+        row = jnp.concatenate(
+            [taps_ref[part : part + 1, :], jnp.zeros((1, 2 * SPAN), jnp.float32)], axis=1
+        )
+        spread = jnp.broadcast_to(row, (SPAN, tap_count + 2 * SPAN))
+        bands.append(pltpu.roll(spread, 0, 1, stride=1, stride_axis=0)[:, :width])
+    real, imag = bands
+    for source, target, band in ((0, 0, real), (0, 1, imag), (1, 0, -imag), (1, 1, real)):
+        high, low = halves_of(band)
+        high_ref[source, target * SPAN : (target + 1) * SPAN, :] = high
+        low_ref[source, target * SPAN : (target + 1) * SPAN, :] = low
+
+
+def band_tables(filter_taps):
+    shape = (2, 2 * SPAN, filter_taps.shape[1] + SPAN)
+    return pl.pallas_call(
+        band_kernel,
+        out_shape=[jax.ShapeDtypeStruct(shape, jnp.bfloat16)] * 2,
+        in_specs=[pl.BlockSpec(memory_space=pltpu.VMEM)],
+        out_specs=[pl.BlockSpec(memory_space=pltpu.VMEM)] * 2,
+        compiler_params=pltpu.CompilerParams(vmem_limit_bytes=32 * MIB),
+    )(filter_taps)
+
+
+def dwell_kernel(
+    sizes,
+    echoes_ref,
+    table_ref,
+    band_high,
+    band_low,
+    out_ref,
+    staged,
+    outgoing,
+    arrived,
+    high_ref,
+    low_ref,
+    rows_ref,
+    load_sem,
+    send_sem,
+    recv_sem,
+    row_send_sem,
+    row_recv_sem,
+):
+    rng_count, chan_count, own, channels, pulses, gates = sizes
+    devices = rng_count * chan_count
+    piece = channels // PIECES
+    block = 2 * piece
+    my_chan = lax.axis_index("chan")
+    my_rng = lax.axis_index("rng")
+    me = my_rng * chan_count + my_chan
+
+    def load(part):
+        return pltpu.make_async_copy(
+            echoes_ref.at[:, pl.ds(part * piece, piece)],
+            staged.at[:, pl.ds(part * piece, piece)],
+            load_sem.at[part],
+        )
+
+    for part in range(PIECES):
+        load(part).start()
+
+    barrier = pltpu.get_barrier_semaphore()
+
+    @pl.loop(1, devices)
+    def _(step):
+        other = lax.rem(me + step, devices)
+        pl.semaphore_signal(
+            barrier,
+            inc=1,
+            device_id={"chan": lax.rem(other, chan_count), "rng": other // chan_count},
+            device_id_type=pl.DeviceIdType.MESH,
+        )
+
+    def chunk(part, bin_index):
+        return outgoing.at[pl.ds((part * pulses + bin_index) * block, block)]
+
+    def send(part, slot):
+        @pl.loop(0, devices - 1)
+        def _(step):
+            offset = devices // 2 + step
+            offset = offset + (offset >= devices).astype(jnp.int32)
+            other = lax.rem(me + offset, devices)
+            pltpu.make_async_remote_copy(
+                src_ref=chunk(part, other * own + slot),
+                dst_ref=arrived.at[slot, part, my_rng, my_chan],
+                send_sem=send_sem.at[part],
+                recv_sem=recv_sem.at[slot, part],
+                device_id={"chan": lax.rem(other, chan_count), "rng": other // chan_count},
+                device_id_type=pl.DeviceIdType.MESH,
+            ).start()
+
+        pltpu.make_async_copy(
+            chunk(part, me * own + slot),
+            arrived.at[slot, part, my_rng, my_chan],
+            recv_sem.at[slot, part],
+        ).start()
+
+    for part in range(PIECES):
+        load(part).wait()
+
+        @pl.loop(0, piece // 8)
+        def _(group):
+            columns = []
+            for lane in range(8):
+                channel = part * piece + group * 8 + lane
+                columns.append(
+                    jnp.concatenate([staged[0, channel], staged[1, channel]], axis=0)
+                )
+            high, low = halves_of(jnp.concatenate(columns, axis=1))
+            spectrum = jnp.dot(
+                table_ref[...],
+                jnp.concatenate([high, high, low], axis=0),
+                preferred_element_type=jnp.float32,
+            )
+            for lane in range(8):
+                first = part * pulses * block + group * 8 + lane
+                outgoing[pl.ds(first, 2 * pulses, stride=piece), :] = spectrum[
+                    :, lane * LANES : (lane + 1) * LANES
+                ]
+
+        if part == 0:
+            pl.semaphore_wait(barrier, devices - 1)
+        send(part, 0)
+    for slot in range(1, own):
+        for part in range(PIECES):
+            send(part, slot)
+
+    spans = gates // SPAN
+    reach = band_high.shape[2] // SPAN
+    per_span = SPAN // LANES
+
+    def finish(slot):
+        @pl.loop(0, PIECES)
+        def _(part):
+            pltpu.make_async_copy(
+                arrived.at[slot, part], arrived.at[slot, part], recv_sem.at[slot, part]
+            ).wait()
+
+            def samples(source, first):
+                columns = []
+                for rng in range(first * per_span, (first + 1) * per_span):
+                    tile = arrived[slot, part, rng, :, pl.ds(source * piece, piece), :]
+                    columns.append(tile.reshape(chan_count * piece, LANES))
+                return halves_of(jnp.concatenate(columns, axis=1))
+
+            pairs = [[samples(source, first) for first in range(spans)] for source in range(2)]
+            for target in range(spans):
+                count = min(reach, spans - target)
+                total = jnp.zeros((chan_count * piece, 2 * SPAN), jnp.float32)
+                for source in range(2):
+                    taken = pairs[source][target : target + count]
+                    high = jnp.concatenate([pair[0] for pair in taken], axis=1)
+                    low = jnp.concatenate([pair[1] for pair in taken], axis=1)
+                    width = count * SPAN
+                    total = total + dot_rows(high, band_high[source, :, :width])
+                    total = total + dot_rows(high, band_low[source, :, :width])
+                    total = total + dot_rows(low, band_high[source, :, :width])
+                high, low = halves_of(total)
+                for chan in range(chan_count):
+                    rows = pl.ds(
+                        pl.multiple_of(chan * channels + part * piece, piece), piece
+                    )
+                    local = slice(chan * piece, (chan + 1) * piece)
+                    for side in range(2):
+                        start = side * gates + target * SPAN
+                        span_cols = slice(side * SPAN, (side + 1) * SPAN)
+                        high_ref[rows, start : start + SPAN] = high[local, span_cols]
+                        low_ref[rows, start : start + SPAN] = low[local, span_cols]
+
+        half = chan_count // 2
+
+        @pl.loop(0, chan_count)
+        def _(step):
+            offset = jnp.where(step < half, half + step, chan_count - 1 - step)
+            owner = lax.rem(my_chan + offset, chan_count)
+            rows = pl.ds(pl.multiple_of(owner * channels, channels), channels)
+
+            def outer(left, right):
+                lefts = slice(left * gates, (left + 1) * gates)
+                rights = slice(right * gates, (right + 1) * gates)
+                total = dot_rows(high_ref[rows, lefts], high_ref[:, rights])
+                total = total + dot_rows(high_ref[rows, lefts], low_ref[:, rights])
+                return total + dot_rows(low_ref[rows, lefts], high_ref[:, rights])
+
+            rows_ref[slot, owner, 0] = (outer(0, 0) + outer(1, 1)) * (1.0 / gates)
+            rows_ref[slot, owner, 1] = (outer(1, 0) - outer(0, 1)) * (1.0 / gates)
+            target_ref = out_ref.at[:, my_chan * own + slot]
+
+            @pl.when(owner != my_chan)
+            def _():
+                pltpu.make_async_remote_copy(
+                    src_ref=rows_ref.at[slot, owner],
+                    dst_ref=target_ref,
+                    send_sem=row_send_sem.at[slot],
+                    recv_sem=row_recv_sem.at[slot],
+                    device_id={"chan": owner, "rng": my_rng},
+                    device_id_type=pl.DeviceIdType.MESH,
+                ).start()
+
+            @pl.when(owner == my_chan)
+            def _():
+                pltpu.make_async_copy(
+                    rows_ref.at[slot, owner], target_ref, row_recv_sem.at[slot]
+                ).start()
+
+    @pl.loop(0, own)
+    def _(slot):
+        finish(slot)
+
+    for part in range(PIECES):
+        sent = outgoing.at[pl.ds(0, (pulses - own) * block)]
+        pltpu.make_async_copy(sent, sent, send_sem.at[part]).wait()
+    for slot in range(own):
+        given = rows_ref.at[slot, pl.ds(0, chan_count - 1)]
+        pltpu.make_async_copy(given, given, row_send_sem.at[slot]).wait()
+        taken = out_ref.at[:, pl.ds(0, chan_count)]
+        pltpu.make_async_copy(taken, taken, row_recv_sem.at[slot]).wait()
+
+
+def by_bins(echoes, filter_taps, rng_count, chan_count):
+    channels, pulses, part = echoes.shape[1:]
+    gates = part * rng_count
+    own = pulses // (rng_count * chan_count)
+    piece = channels // PIECES
+    whole = channels * chan_count
+    sizes = (rng_count, chan_count, own, channels, pulses, gates)
+    band_high, band_low = band_tables(filter_taps)
+    vmem = pl.BlockSpec(memory_space=pltpu.VMEM)
+    hbm = pl.BlockSpec(memory_space=pl.ANY)
+    return pl.pallas_call(
+        functools.partial(dwell_kernel, sizes),
+        out_shape=jax.ShapeDtypeStruct((2, own * chan_count, channels, whole), jnp.float32),
+        in_specs=[hbm, vmem, vmem, vmem],
+        out_specs=hbm,
+        scratch_shapes=[
+            pltpu.VMEM(echoes.shape, jnp.float32),
+            pltpu.VMEM((2 * pulses * channels, part), jnp.float32),
+            pltpu.VMEM((own, PIECES, rng_count, chan_count, 2 * piece, part), jnp.float32),
+            pltpu.VMEM((whole, 2 * gates), jnp.bfloat16),
+            pltpu.VMEM((whole, 2 * gates), jnp.bfloat16),
+            pltpu.VMEM((own, chan_count, 2, channels, whole), jnp.float32),
+            pltpu.SemaphoreType.DMA((PIECES,)),
+            pltpu.SemaphoreType.DMA((PIECES,)),
+            pltpu.SemaphoreType.DMA((own, PIECES)),
+            pltpu.SemaphoreType.DMA((own,)),
+            pltpu.SemaphoreType.DMA((own,)),
+        ],
+        compiler_params=pltpu.CompilerParams(
+            collective_id=0, has_side_effects=True, vmem_limit_bytes=56 * MIB
+        ),
+    )(echoes, jnp.asarray(doppler_table(pulses)), band_high, band_low)
+
+
 def solution(mesh):
+    rng_count = mesh.shape["rng"]
+    chan_count = mesh.shape["chan"]
+
+    def per_device(echoes, filter_taps):
+        channels, pulses, part = echoes.shape[1:]
+        fits = (
+            pulses % (rng_count * chan_count) == 0
+            and part == LANES
+            and (part * rng_count) % SPAN == 0
+            and filter_taps.shape[1] % SPAN == 0
+            and channels % (16 * PIECES) == 0
+        )
+        if fits:
+            return by_bins(echoes, filter_taps, rng_count, chan_count)
+        return by_gates(echoes, filter_taps)
+
     in_specs = (P(None, "chan", None, "rng"), P())
     out_specs = P(None, "rng", "chan", None)
     return jax.shard_map(

time: 1040 us -> 235 us (0.23)
  blocking collectives: 471 us -> 0 us
  waiting for transfers between devices: 278 us -> 0 us
  Pallas kernels: 0 us -> 227 us
  matrix products: 119 us -> 0 us
  local copies, waits for them, and re-layouts: 114 us -> 7.82 us
  other arithmetic: 29.5 us -> 0 us
  between operations: 14.1 us -> 0.03 us
    all_to_all x3 -> x0, blocking collectives: 471 us -> none  [the longest x1 187 us: per_device(): lax.all_to_all(filtered, 'rng', split_axis=3, concat_axis=2, tiled=True)]
    pallas_call x0 -> x2, Pallas kernels: none -> 227 us  [the longest x1 227 us: by_bins(): pl.pallas_call(functools.partial(dwell_kernel, sizes), out_shape=jax.Shap...]
    all_to_all x1 -> x0, waiting for transfers between devices: 156 us -> none  [per_device(): lax.all_to_all(echoes, 'rng', split_axis=2, concat_axis=3, tiled=True)]
    reduce_scatter x2 -> x0, waiting for transfers between devices: 123 us -> none  [the longest x1 74.5 us: per_device(): lax.psum_scatter(real_part, 'chan', scatter_dimension=1, tiled=True)]
    dot_general x7 -> x0, matrix products: 119 us -> none  [the longest x1 62 us: range_filter(): jnp.einsum('abnw,sow->sabno', joined, both_tables, precision=lax.Precisio...]
    all_to_all x4 -> x0, local copies, waits for them, and re-layouts: 29.3 us -> none  [the longest x1 9.19 us: per_device(): lax.all_to_all(spectrum, 'rng', split_axis=2, concat_axis=3, tiled=True)]
    slice x7 -> x0, local copies, waits for them, and re-layouts: 27 us -> none  [the longest x2 9.25 us: per_device(): spec_re = gathered[0]]
    unnamed x13 -> x7, local copies, waits for them, and re-layouts: 30.9 us -> 7.82 us
  transfers between devices with their start and end apart: 3 -> 0, of which waited for: 3 -> 0; matrix products, arithmetic and copies ran while one was open for 5% -> 0% of each run, Pallas kernels for 0% -> 0%
where the time goes in v2:
time: 235 us
  Pallas kernels  227 us (97%)
  local copies, waits for them, and re-layouts  7.82 us (3%)
    pallas_call x1, Pallas kernels, by_bins(): pl.pallas_call(functools.partial(dwell_kernel, sizes), out_shape=jax.Shap...  227 us
    unnamed x7, local copies, waits for them, and re-layouts  7.82 us

profile of v2, /device:TPU:0, one launch (start us, length us, event | category | flops | bytes accessed | tf_op | source)
XLA Modules:
  0.0 234.8 jit_solution(12394271700362119974)
XLA Ops:
  0.0 0.0 copy-start.2
  0.0 0.7 copy-done.2
  0.7 0.3 shard_map.37
  1.0 0.0 copy-start
  1.0 1.1 copy-done
  2.2 0.0 copy-start.1
  2.2 1.2 copy-done.1
  3.3 226.6 %shard_map.38 = f32[2,8,128,512]{3,2,1,0:T(8,128)} custom-call(f32[2,128,64,128]{3,2,1,0:T(8,128)} %echoes_ref.1, bf16[128,384]{1,0:T(8,128)(2,1)} %constant.2.clone.table_ref, bf16[2,512,768]{2,1,0:T(8,128)(2,1)} %copy-done, bf16[2,512,768]{2,1,0:T(8,128)(2,1)} %copy-done.1), custom_call_target="tpu_custom_call" | custom-call | tf_op jit(solution)/shard_map/pallas_call | solution.py:373
  230.0 4.8 %copy.5 = f32[2,8,128,512]{3,2,1,0:T(8,128)} copy(f32[2,8,128,512]{3,2,1,0:T(8,128)} %shard_map.38) | data formatting | bytes 8388608
Async XLA Ops:
  0.0 0.7 copy-start.2
  1.0 1.1 copy-start
  2.2 1.2 copy-start.1

commit v3 on v2

--- a/solution.py
+++ b/solution.py
@@ -103,7 +103,7 @@
 
 SPAN = 256
 LANES = 128
-PIECES = 2
+SUBS = 4
 MIB = 2**20
 
 
@@ -117,7 +117,7 @@
             np.concatenate([cos_table, sin_table], axis=1),
             np.concatenate([-sin_table, cos_table], axis=1),
         ],
-        axis=1,
+        axis=0,
     )
     table = rows.reshape(2 * pulse_count, 2 * pulse_count).astype(np.float32)
     high = table.astype(ml_dtypes.bfloat16)
@@ -178,29 +178,37 @@
     high_ref,
     low_ref,
     rows_ref,
+    early_ref,
+    edge_ref,
+    late_ref,
     load_sem,
     send_sem,
     recv_sem,
     row_send_sem,
     row_recv_sem,
+    early_sem,
+    late_sem,
 ):
     rng_count, chan_count, own, channels, pulses, gates = sizes
     devices = rng_count * chan_count
-    piece = channels // PIECES
-    block = 2 * piece
+    small = channels // SUBS
+    big = channels - small
+    pieces = ((0, small), (small, big))
+    last = own - 1
     my_chan = lax.axis_index("chan")
     my_rng = lax.axis_index("rng")
     me = my_rng * chan_count + my_chan
 
-    def load(part):
+    def load(index):
+        first, count = pieces[index]
         return pltpu.make_async_copy(
-            echoes_ref.at[:, pl.ds(part * piece, piece)],
-            staged.at[:, pl.ds(part * piece, piece)],
-            load_sem.at[part],
-        )
-
-    for part in range(PIECES):
-        load(part).start()
+            echoes_ref.at[:, pl.ds(first, count)],
+            staged.at[:, pl.ds(first, count)],
+            load_sem.at[index],
+        )
+
+    for index in range(2):
+        load(index).start()
 
     barrier = pltpu.get_barrier_semaphore()
 
@@ -214,38 +222,41 @@
             device_id_type=pl.DeviceIdType.MESH,
         )
 
-    def chunk(part, bin_index):
-        return outgoing.at[pl.ds((part * pulses + bin_index) * block, block)]
-
-    def send(part, slot):
+    def chunk(index, bin_index):
+        first, count = pieces[index]
+        return outgoing.at[pl.ds(2 * (first * pulses + bin_index * count), 2 * count)]
+
+    def landing(index, slot):
+        first, count = pieces[index]
+        return arrived.at[slot, my_rng, my_chan, pl.ds(2 * first, 2 * count)]
+
+    def send(index, slot):
         @pl.loop(0, devices - 1)
         def _(step):
             offset = devices // 2 + step
             offset = offset + (offset >= devices).astype(jnp.int32)
             other = lax.rem(me + offset, devices)
             pltpu.make_async_remote_copy(
-                src_ref=chunk(part, other * own + slot),
-                dst_ref=arrived.at[slot, part, my_rng, my_chan],
-                send_sem=send_sem.at[part],
-                recv_sem=recv_sem.at[slot, part],
+                src_ref=chunk(index, other * own + slot),
+                dst_ref=landing(index, slot),
+                send_sem=send_sem.at[index],
+                recv_sem=recv_sem.at[slot, index],
                 device_id={"chan": lax.rem(other, chan_count), "rng": other // chan_count},
                 device_id_type=pl.DeviceIdType.MESH,
             ).start()
 
         pltpu.make_async_copy(
-            chunk(part, me * own + slot),
-            arrived.at[slot, part, my_rng, my_chan],
-            recv_sem.at[slot, part],
+            chunk(index, me * own + slot), landing(index, slot), recv_sem.at[slot, index]
         ).start()
 
-    for part in range(PIECES):
-        load(part).wait()
-
-        @pl.loop(0, piece // 8)
+    def transform(index):
+        first, count = pieces[index]
+
+        @pl.loop(0, count // 8)
         def _(group):
             columns = []
             for lane in range(8):
-                channel = part * piece + group * 8 + lane
+                channel = first + group * 8 + lane
                 columns.append(
                     jnp.concatenate([staged[0, channel], staged[1, channel]], axis=0)
                 )
@@ -255,116 +266,236 @@
                 jnp.concatenate([high, high, low], axis=0),
                 preferred_element_type=jnp.float32,
             )
-            for lane in range(8):
-                first = part * pulses * block + group * 8 + lane
-                outgoing[pl.ds(first, 2 * pulses, stride=piece), :] = spectrum[
-                    :, lane * LANES : (lane + 1) * LANES
-                ]
-
-        if part == 0:
+            sub = group // (small // 8)
+            place = sub * 2 * small + (group - sub * (small // 8)) * 8
+            for side in range(2):
+                for lane in range(8):
+                    start = 2 * first * pulses + side * small + place + lane
+                    outgoing[pl.ds(start, pulses, stride=2 * count), :] = spectrum[
+                        side * pulses : (side + 1) * pulses,
+                        lane * LANES : (lane + 1) * LANES,
+                    ]
+
+    for index in range(2):
+        load(index).wait()
+        transform(index)
+        if index == 0:
             pl.semaphore_wait(barrier, devices - 1)
-        send(part, 0)
+        send(index, 0)
     for slot in range(1, own):
-        for part in range(PIECES):
-            send(part, slot)
+        for index in (1, 0):
+            send(index, slot)
 
     spans = gates // SPAN
     reach = band_high.shape[2] // SPAN
     per_span = SPAN // LANES
 
-    def finish(slot):
-        @pl.loop(0, PIECES)
-        def _(part):
-            pltpu.make_async_copy(
-                arrived.at[slot, part], arrived.at[slot, part], recv_sem.at[slot, part]
-            ).wait()
-
-            def samples(source, first):
-                columns = []
-                for rng in range(first * per_span, (first + 1) * per_span):
-                    tile = arrived[slot, part, rng, :, pl.ds(source * piece, piece), :]
-                    columns.append(tile.reshape(chan_count * piece, LANES))
-                return halves_of(jnp.concatenate(columns, axis=1))
-
-            pairs = [[samples(source, first) for first in range(spans)] for source in range(2)]
-            for target in range(spans):
-                count = min(reach, spans - target)
-                total = jnp.zeros((chan_count * piece, 2 * SPAN), jnp.float32)
-                for source in range(2):
-                    taken = pairs[source][target : target + count]
-                    high = jnp.concatenate([pair[0] for pair in taken], axis=1)
-                    low = jnp.concatenate([pair[1] for pair in taken], axis=1)
-                    width = count * SPAN
-                    total = total + dot_rows(high, band_high[source, :, :width])
-                    total = total + dot_rows(high, band_low[source, :, :width])
-                    total = total + dot_rows(low, band_high[source, :, :width])
-                high, low = halves_of(total)
-                for chan in range(chan_count):
-                    rows = pl.ds(
-                        pl.multiple_of(chan * channels + part * piece, piece), piece
-                    )
-                    local = slice(chan * piece, (chan + 1) * piece)
-                    for side in range(2):
-                        start = side * gates + target * SPAN
-                        span_cols = slice(side * SPAN, (side + 1) * SPAN)
-                        high_ref[rows, start : start + SPAN] = high[local, span_cols]
-                        low_ref[rows, start : start + SPAN] = low[local, span_cols]
-
+    def receive(index, slot):
+        first, count = pieces[index]
+        landed = arrived.at[slot, :, :, pl.ds(2 * first, 2 * count)]
+        pltpu.make_async_copy(landed, landed, recv_sem.at[slot, index]).wait()
+
+    def convolve(sub, slot):
+        def samples(source, first):
+            columns = []
+            for rng in range(first * per_span, (first + 1) * per_span):
+                rows = pl.ds(pl.multiple_of((2 * sub + source) * small, small), small)
+                tile = arrived[slot, rng, :, rows, :]
+                columns.append(tile.reshape(chan_count * small, LANES))
+            return halves_of(jnp.concatenate(columns, axis=1))
+
+        pairs = [[samples(source, first) for first in range(spans)] for source in range(2)]
+        for target in range(spans):
+            count = min(reach, spans - target)
+            total = jnp.zeros((chan_count * small, 2 * SPAN), jnp.float32)
+            for source in range(2):
+                taken = pairs[source][target : target + count]
+                high = jnp.concatenate([pair[0] for pair in taken], axis=1)
+                low = jnp.concatenate([pair[1] for pair in taken], axis=1)
+                width = count * SPAN
+                total = total + dot_rows(high, band_high[source, :, :width])
+                total = total + dot_rows(high, band_low[source, :, :width])
+                total = total + dot_rows(low, band_high[source, :, :width])
+            high, low = halves_of(total)
+            for chan in range(chan_count):
+                rows = pl.ds(pl.multiple_of(chan * channels + sub * small, small), small)
+                local = slice(chan * small, (chan + 1) * small)
+                for side in range(2):
+                    start = side * gates + target * SPAN
+                    span_cols = slice(side * SPAN, (side + 1) * SPAN)
+                    high_ref[rows, start : start + SPAN] = high[local, span_cols]
+                    low_ref[rows, start : start + SPAN] = low[local, span_cols]
+
+    def outer(left, right):
+        def one(first, second):
+            lefts = slice(first * gates, (first + 1) * gates)
+            rights = slice(second * gates, (second + 1) * gates)
+            total = dot_rows(left[0](lefts), right[0](rights))
+            total = total + dot_rows(left[0](lefts), right[1](rights))
+            return total + dot_rows(left[1](lefts), right[0](rights))
+
+        scale = 1.0 / gates
+        return (one(0, 0) + one(1, 1)) * scale, (one(1, 0) - one(0, 1)) * scale
+
+    def rows_of(first, count):
+        rows = pl.ds(pl.multiple_of(first, small), count)
+        return tuple(lambda cols, ref=ref: ref[rows, cols] for ref in (high_ref, low_ref))
+
+    every = tuple(lambda cols, ref=ref: ref[:, cols] for ref in (high_ref, low_ref))
+
+    def edge(cols, ref):
+        return jnp.concatenate(
+            [ref[chan * channels : chan * channels + small, cols] for chan in range(chan_count)],
+            axis=0,
+        )
+
+    edges = tuple(lambda cols, ref=ref: edge(cols, ref) for ref in (high_ref, low_ref))
+
+    def owner_at(step):
         half = chan_count // 2
+        offset = jnp.where(step < half, half + step, chan_count - 1 - step)
+        return lax.rem(my_chan + offset, chan_count)
+
+    def hand_over(owner, source, target, send_to, recv_from):
+        @pl.when(owner != my_chan)
+        def _():
+            pltpu.make_async_remote_copy(
+                src_ref=source,
+                dst_ref=target,
+                send_sem=send_to,
+                recv_sem=recv_from,
+                device_id={"chan": owner, "rng": my_rng},
+                device_id_type=pl.DeviceIdType.MESH,
+            ).start()
+
+        @pl.when(owner == my_chan)
+        def _():
+            pltpu.make_async_copy(source, target, recv_from).start()
+
+    for slot in range(last):
+        receive(0, slot)
+        convolve(0, slot)
+        receive(1, slot)
+
+        @pl.loop(1, SUBS)
+        def _(sub):
+            convolve(sub, slot)
 
         @pl.loop(0, chan_count)
         def _(step):
-            offset = jnp.where(step < half, half + step, chan_count - 1 - step)
-            owner = lax.rem(my_chan + offset, chan_count)
-            rows = pl.ds(pl.multiple_of(owner * channels, channels), channels)
-
-            def outer(left, right):
-                lefts = slice(left * gates, (left + 1) * gates)
-                rights = slice(right * gates, (right + 1) * gates)
-                total = dot_rows(high_ref[rows, lefts], high_ref[:, rights])
-                total = total + dot_rows(high_ref[rows, lefts], low_ref[:, rights])
-                return total + dot_rows(low_ref[rows, lefts], high_ref[:, rights])
-
-            rows_ref[slot, owner, 0] = (outer(0, 0) + outer(1, 1)) * (1.0 / gates)
-            rows_ref[slot, owner, 1] = (outer(1, 0) - outer(0, 1)) * (1.0 / gates)
-            target_ref = out_ref.at[:, my_chan * own + slot]
-
-            @pl.when(owner != my_chan)
-            def _():
-                pltpu.make_async_remote_copy(
-                    src_ref=rows_ref.at[slot, owner],
-                    dst_ref=target_ref,
-                    send_sem=row_send_sem.at[slot],
-                    recv_sem=row_recv_sem.at[slot],
-                    device_id={"chan": owner, "rng": my_rng},
-                    device_id_type=pl.DeviceIdType.MESH,
-                ).start()
-
-            @pl.when(owner == my_chan)
-            def _():
-                pltpu.make_async_copy(
-                    rows_ref.at[slot, owner], target_ref, row_recv_sem.at[slot]
-                ).start()
-
-    @pl.loop(0, own)
-    def _(slot):
-        finish(slot)
-
-    for part in range(PIECES):
-        sent = outgoing.at[pl.ds(0, (pulses - own) * block)]
-        pltpu.make_async_copy(sent, sent, send_sem.at[part]).wait()
-    for slot in range(own):
-        given = rows_ref.at[slot, pl.ds(0, chan_count - 1)]
+            owner = owner_at(step)
+            real, imag = outer(rows_of(owner * channels, channels), every)
+            rows_ref[slot, owner, 0] = real
+            rows_ref[slot, owner, 1] = imag
+            hand_over(
+                owner,
+                rows_ref.at[slot, owner],
+                out_ref.at[:, my_chan * own + slot],
+                row_send_sem.at[slot],
+                row_recv_sem.at[slot],
+            )
+
+    receive(1, last)
+
+    @pl.loop(1, SUBS)
+    def _(sub):
+        convolve(sub, last)
+
+    @pl.loop(0, chan_count)
+    def _(step):
+        owner = owner_at(step)
+        real, imag = outer(rows_of(owner * channels + small, big), every)
+        rows_ref[last, owner, 0, small:, :] = real
+        rows_ref[last, owner, 1, small:, :] = imag
+        hand_over(
+            owner,
+            rows_ref.at[last, owner, :, pl.ds(small, big)],
+            early_ref.at[my_chan],
+            early_sem.at[0],
+            early_sem.at[1],
+        )
+
+    receive(0, last)
+    convolve(0, last)
+    real, imag = outer(edges, every)
+    for chan in range(chan_count):
+        local = slice(chan * small, (chan + 1) * small)
+        rows_ref[last, chan, 0, :small, :] = real[local]
+        rows_ref[last, chan, 1, :small, :] = imag[local]
+
+    @pl.loop(0, chan_count)
+    def _(step):
+        owner = owner_at(step)
+        hand_over(
+            owner,
+            rows_ref.at[last, owner, :, pl.ds(0, small)],
+            out_ref.at[:, my_chan * own + last, pl.ds(0, small)],
+            row_send_sem.at[last],
+            row_recv_sem.at[last],
+        )
+
+    @pl.loop(0, chan_count)
+    def _(step):
+        owner = owner_at(step)
+        real, imag = outer(rows_of(owner * channels + small, big), edges)
+        edge_ref[owner, 0] = real
+        edge_ref[owner, 1] = imag
+        hand_over(
+            owner, edge_ref.at[owner], late_ref.at[my_chan], late_sem.at[0], late_sem.at[1]
+        )
+
+    pltpu.make_async_copy(early_ref, early_ref, early_sem.at[1]).wait()
+    pltpu.make_async_copy(late_ref, late_ref, late_sem.at[1]).wait()
+    width = chan_count * small
+    lanes = lax.broadcasted_iota(jnp.int32, (big, width), 1)
+    for chan in range(chan_count):
+        for side in range(2):
+            late = late_ref[chan, side]
+            for tile in range(chan_count):
+                cols = slice(tile * channels, (tile + 1) * channels)
+                moved = pltpu.roll(late, (width - tile * small) % width, 1)
+                early_ref[chan, side, :, cols] = jnp.where(
+                    lanes < small, moved, early_ref[chan, side, :, cols]
+                )
+
+    def deliver(chan):
+        return pltpu.make_async_copy(
+            early_ref.at[chan],
+            out_ref.at[:, chan * own + last, pl.ds(small, big)],
+            load_sem.at[chan],
+        )
+
+    for chan in range(chan_count):
+        deliver(chan).start()
+    for index in range(2):
+        first, count = pieces[index]
+        sent = outgoing.at[pl.ds(0, 2 * (pulses - own) * count)]
+        pltpu.make_async_copy(sent, sent, send_sem.at[index]).wait()
+    others = pl.ds(0, chan_count - 1)
+    bins = pl.ds(0, chan_count)
+    for slot in range(last):
+        given = rows_ref.at[slot, others]
         pltpu.make_async_copy(given, given, row_send_sem.at[slot]).wait()
-        taken = out_ref.at[:, pl.ds(0, chan_count)]
+        taken = out_ref.at[:, bins]
         pltpu.make_async_copy(taken, taken, row_recv_sem.at[slot]).wait()
+    given = rows_ref.at[last, others, :, pl.ds(0, small)]
+    pltpu.make_async_copy(given, given, row_send_sem.at[last]).wait()
+    taken = out_ref.at[:, bins, pl.ds(0, small)]
+    pltpu.make_async_copy(taken, taken, row_recv_sem.at[last]).wait()
+    given = early_ref.at[others]
+    pltpu.make_async_copy(given, given, early_sem.at[0]).wait()
+    given = edge_ref.at[others]
+    pltpu.make_async_copy(given, given, late_sem.at[0]).wait()
+    for chan in range(chan_count):
+        deliver(chan).wait()
 
 
 def by_bins(echoes, filter_taps, rng_count, chan_count):
     channels, pulses, part = echoes.shape[1:]
     gates = part * rng_count
     own = pulses // (rng_count * chan_count)
-    piece = channels // PIECES
+    small = channels // SUBS
+    big = channels - small
     whole = channels * chan_count
     sizes = (rng_count, chan_count, own, channels, pulses, gates)
     band_high, band_low = band_tables(filter_taps)
@@ -378,15 +509,20 @@
         scratch_shapes=[
             pltpu.VMEM(echoes.shape, jnp.float32),
             pltpu.VMEM((2 * pulses * channels, part), jnp.float32),
-            pltpu.VMEM((own, PIECES, rng_count, chan_count, 2 * piece, part), jnp.float32),
+            pltpu.VMEM((own, rng_count, chan_count, 2 * channels, part), jnp.float32),
             pltpu.VMEM((whole, 2 * gates), jnp.bfloat16),
             pltpu.VMEM((whole, 2 * gates), jnp.bfloat16),
             pltpu.VMEM((own, chan_count, 2, channels, whole), jnp.float32),
-            pltpu.SemaphoreType.DMA((PIECES,)),
-            pltpu.SemaphoreType.DMA((PIECES,)),
-            pltpu.SemaphoreType.DMA((own, PIECES)),
+            pltpu.VMEM((chan_count, 2, big, whole), jnp.float32),
+            pltpu.VMEM((chan_count, 2, big, chan_count * small), jnp.float32),
+            pltpu.VMEM((chan_count, 2, big, chan_count * small), jnp.float32),
+            pltpu.SemaphoreType.DMA((max(2, chan_count),)),
+            pltpu.SemaphoreType.DMA((2,)),
+            pltpu.SemaphoreType.DMA((own, 2)),
             pltpu.SemaphoreType.DMA((own,)),
             pltpu.SemaphoreType.DMA((own,)),
+            pltpu.SemaphoreType.DMA((2,)),
+            pltpu.SemaphoreType.DMA((2,)),
         ],
         compiler_params=pltpu.CompilerParams(
             collective_id=0, has_side_effects=True, vmem_limit_bytes=56 * MIB
@@ -402,10 +538,12 @@
         channels, pulses, part = echoes.shape[1:]
         fits = (
             pulses % (rng_count * chan_count) == 0
+            and pulses >= 2 * rng_count * chan_count
+            and chan_count == SUBS
+            and channels == LANES
             and part == LANES
             and (part * rng_count) % SPAN == 0
             and filter_taps.shape[1] % SPAN == 0
-            and channels % (16 * PIECES) == 0
         )
         if fits:
             return by_bins(echoes, filter_taps, rng_count, chan_count)

time: 235 us -> 240 us (1.021)
  Pallas kernels: 227 us -> 232 us
    pallas_call x1, Pallas kernels: 227 us -> 232 us  [by_bins(): pl.pallas_call(functools.partial(dwell_kernel, sizes), out_shape=jax.Shap...]
where the time goes in v3:
time: 240 us
  Pallas kernels  232 us (97%)
  local copies, waits for them, and re-layouts  7.82 us (3%)
    pallas_call x1, Pallas kernels, by_bins(): pl.pallas_call(functools.partial(dwell_kernel, sizes), out_shape=jax.Shap...  232 us
    unnamed x7, local copies, waits for them, and re-layouts  7.82 us

profile of v3, /device:TPU:0, one launch (start us, length us, event | category | flops | bytes accessed | tf_op | source)
XLA Modules:
  0.0 240.3 jit_solution(18283232559134517981)
XLA Ops:
  0.0 0.0 copy-start.2
  0.0 0.7 copy-done.2
  0.7 0.3 shard_map.37
  1.0 0.0 copy-start
  1.0 1.1 copy-done
  2.2 0.0 copy-start.1
  2.2 1.2 copy-done.1
  3.3 232.1 %shard_map.38 = f32[2,8,128,512]{3,2,1,0:T(8,128)} custom-call(f32[2,128,64,128]{3,2,1,0:T(8,128)} %echoes_ref.1, bf16[128,384]{1,0:T(8,128)(2,1)} %constant.2.clone.table_ref, bf16[2,512,768]{2,1,0:T(8,128)(2,1)} %copy-done, bf16[2,512,768]{2,1,0:T(8,128)(2,1)} %copy-done.1), custom_call_target="tpu_custom_call" | custom-call | tf_op jit(solution)/shard_map/pallas_call | solution.py:504
  235.5 4.8 %copy.5 = f32[2,8,128,512]{3,2,1,0:T(8,128)} copy(f32[2,8,128,512]{3,2,1,0:T(8,128)} %shard_map.38) | data formatting | bytes 8388608
Async XLA Ops:
  0.0 0.7 copy-start.2
  1.0 1.1 copy-start
  2.2 1.2 copy-start.1

commit v4 on v3

--- a/solution.py
+++ b/solution.py
@@ -104,6 +104,7 @@
 SPAN = 256
 LANES = 128
 SUBS = 4
+WINDOW = 3
 MIB = 2**20
 
 
@@ -222,41 +223,53 @@
             device_id_type=pl.DeviceIdType.MESH,
         )
 
-    def chunk(index, bin_index):
-        first, count = pieces[index]
-        return outgoing.at[pl.ds(2 * (first * pulses + bin_index * count), 2 * count)]
-
-    def landing(index, slot):
-        first, count = pieces[index]
-        return arrived.at[slot, my_rng, my_chan, pl.ds(2 * first, 2 * count)]
-
-    def send(index, slot):
+    block = 2 * small
+
+    def chunk(sub, bin_index):
+        start = pl.multiple_of((sub * pulses + bin_index) * block, block)
+        return outgoing.at[pl.ds(start, block)]
+
+    def landing(sub, slot):
+        rows = pl.ds(pl.multiple_of(sub * block, block), block)
+        return arrived.at[slot, my_rng, my_chan, rows]
+
+    def turn(phase):
+        slot = phase // SUBS
+        place = phase - slot * SUBS
+        return slot, lax.rem(place + slot // last, SUBS)
+
+    def send(phase):
+        slot, sub = turn(phase)
+
         @pl.loop(0, devices - 1)
         def _(step):
             offset = devices // 2 + step
             offset = offset + (offset >= devices).astype(jnp.int32)
             other = lax.rem(me + offset, devices)
             pltpu.make_async_remote_copy(
-                src_ref=chunk(index, other * own + slot),
-                dst_ref=landing(index, slot),
-                send_sem=send_sem.at[index],
-                recv_sem=recv_sem.at[slot, index],
+                src_ref=chunk(sub, other * own + slot),
+                dst_ref=landing(sub, slot),
+                send_sem=send_sem.at[slot, sub],
+                recv_sem=recv_sem.at[slot, sub],
                 device_id={"chan": lax.rem(other, chan_count), "rng": other // chan_count},
                 device_id_type=pl.DeviceIdType.MESH,
             ).start()
 
         pltpu.make_async_copy(
-            chunk(index, me * own + slot), landing(index, slot), recv_sem.at[slot, index]
+            chunk(sub, me * own + slot), landing(sub, slot), recv_sem.at[slot, sub]
         ).start()
 
-    def transform(index):
-        first, count = pieces[index]
-
-        @pl.loop(0, count // 8)
+    def wait_sent(phase):
+        slot, sub = turn(phase)
+        sent = outgoing.at[pl.ds(0, (devices - 1) * block)]
+        pltpu.make_async_copy(sent, sent, send_sem.at[slot, sub]).wait()
+
+    def transform(sub):
+        @pl.loop(0, small // 8)
         def _(group):
             columns = []
             for lane in range(8):
-                channel = first + group * 8 + lane
+                channel = sub * small + group * 8 + lane
                 columns.append(
                     jnp.concatenate([staged[0, channel], staged[1, channel]], axis=0)
                 )
@@ -266,34 +279,41 @@
                 jnp.concatenate([high, high, low], axis=0),
                 preferred_element_type=jnp.float32,
             )
-            sub = group // (small // 8)
-            place = sub * 2 * small + (group - sub * (small // 8)) * 8
             for side in range(2):
                 for lane in range(8):
-                    start = 2 * first * pulses + side * small + place + lane
-                    outgoing[pl.ds(start, pulses, stride=2 * count), :] = spectrum[
+                    start = sub * pulses * block + side * small + group * 8 + lane
+                    outgoing[pl.ds(start, pulses, stride=block), :] = spectrum[
                         side * pulses : (side + 1) * pulses,
                         lane * LANES : (lane + 1) * LANES,
                     ]
 
-    for index in range(2):
-        load(index).wait()
-        transform(index)
-        if index == 0:
+    for sub in range(SUBS):
+        if sub < 2:
+            load(sub).wait()
+        transform(sub)
+        if sub == 0:
             pl.semaphore_wait(barrier, devices - 1)
-        send(index, 0)
-    for slot in range(1, own):
-        for index in (1, 0):
-            send(index, slot)
+        if sub < WINDOW:
+            send(jnp.int32(sub))
+
+    phases = own * SUBS
+
+    def advance(phase):
+        wait_sent(phase)
+
+        @pl.when(phase + WINDOW < phases)
+        def _():
+            send(phase + WINDOW)
+
+        slot, sub = turn(phase)
+        rows = pl.ds(pl.multiple_of(sub * block, block), block)
+        landed = arrived.at[slot, :, :, rows]
+        pltpu.make_async_copy(landed, landed, recv_sem.at[slot, sub]).wait()
+        convolve(sub, slot)
 
     spans = gates // SPAN
     reach = band_high.shape[2] // SPAN
     per_span = SPAN // LANES
-
-    def receive(index, slot):
-        first, count = pieces[index]
-        landed = arrived.at[slot, :, :, pl.ds(2 * first, 2 * count)]
-        pltpu.make_async_copy(landed, landed, recv_sem.at[slot, index]).wait()
 
     def convolve(sub, slot):
         def samples(source, first):
@@ -373,13 +393,9 @@
             pltpu.make_async_copy(source, target, recv_from).start()
 
     for slot in range(last):
-        receive(0, slot)
-        convolve(0, slot)
-        receive(1, slot)
-
-        @pl.loop(1, SUBS)
-        def _(sub):
-            convolve(sub, slot)
+        @pl.loop(slot * SUBS, (slot + 1) * SUBS)
+        def _(phase):
+            advance(phase)
 
         @pl.loop(0, chan_count)
         def _(step):
@@ -395,11 +411,9 @@
                 row_recv_sem.at[slot],
             )
 
-    receive(1, last)
-
-    @pl.loop(1, SUBS)
-    def _(sub):
-        convolve(sub, last)
+    @pl.loop(last * SUBS, phases - 1)
+    def _(phase):
+        advance(phase)
 
     @pl.loop(0, chan_count)
     def _(step):
@@ -415,8 +429,7 @@
             early_sem.at[1],
         )
 
-    receive(0, last)
-    convolve(0, last)
+    advance(jnp.int32(phases - 1))
     real, imag = outer(edges, every)
     for chan in range(chan_count):
         local = slice(chan * small, (chan + 1) * small)
@@ -467,10 +480,6 @@
 
     for chan in range(chan_count):
         deliver(chan).start()
-    for index in range(2):
-        first, count = pieces[index]
-        sent = outgoing.at[pl.ds(0, 2 * (pulses - own) * count)]
-        pltpu.make_async_copy(sent, sent, send_sem.at[index]).wait()
     others = pl.ds(0, chan_count - 1)
     bins = pl.ds(0, chan_count)
     for slot in range(last):
@@ -517,8 +526,8 @@
             pltpu.VMEM((chan_count, 2, big, chan_count * small), jnp.float32),
             pltpu.VMEM((chan_count, 2, big, chan_count * small), jnp.float32),
             pltpu.SemaphoreType.DMA((max(2, chan_count),)),
-            pltpu.SemaphoreType.DMA((2,)),
-            pltpu.SemaphoreType.DMA((own, 2)),
+            pltpu.SemaphoreType.DMA((own, SUBS)),
+            pltpu.SemaphoreType.DMA((own, SUBS)),
             pltpu.SemaphoreType.DMA((own,)),
             pltpu.SemaphoreType.DMA((own,)),
             pltpu.SemaphoreType.DMA((2,)),

time: 240 us -> 232 us (0.967)
  Pallas kernels: 232 us -> 224 us
    pallas_call x1, Pallas kernels: 232 us -> 224 us  [by_bins(): pl.pallas_call(functools.partial(dwell_kernel, sizes), out_shape=jax.Shap...]
where the time goes in v4:
time: 232 us
  Pallas kernels  224 us (97%)
  local copies, waits for them, and re-layouts  7.82 us (3%)
    pallas_call x1, Pallas kernels, by_bins(): pl.pallas_call(functools.partial(dwell_kernel, sizes), out_shape=jax.Shap...  224 us
    unnamed x7, local copies, waits for them, and re-layouts  7.82 us

profile of v4, /device:TPU:0, one launch (start us, length us, event | category | flops | bytes accessed | tf_op | source)
XLA Modules:
  0.0 231.7 jit_solution(5176608539792894042)
XLA Ops:
  0.0 0.0 copy-start.2
  0.0 0.7 copy-done.2
  0.7 0.3 shard_map.37
  1.0 0.0 copy-start
  1.0 1.1 copy-done
  2.2 0.0 copy-start.1
  2.2 1.2 copy-done.1
  3.3 223.5 %shard_map.38 = f32[2,8,128,512]{3,2,1,0:T(8,128)} custom-call(f32[2,128,64,128]{3,2,1,0:T(8,128)} %echoes_ref.1, bf16[128,384]{1,0:T(8,128)(2,1)} %constant.2.clone.table_ref, bf16[2,512,768]{2,1,0:T(8,128)(2,1)} %copy-done, bf16[2,512,768]{2,1,0:T(8,128)(2,1)} %copy-done.1), custom_call_target="tpu_custom_call" | custom-call | tf_op jit(solution)/shard_map/pallas_call | solution.py:513
  226.9 4.8 %copy.5 = f32[2,8,128,512]{3,2,1,0:T(8,128)} copy(f32[2,8,128,512]{3,2,1,0:T(8,128)} %shard_map.38) | data formatting | bytes 8388608
Async XLA Ops:
  0.0 0.7 copy-start.2
  1.0 1.1 copy-start
  2.2 1.2 copy-start.1
